TPU v7x, 128 devices: a whole 4x4x4 slice. The times are simulated.
128 devices in a mesh: dp: 32 (over y_hi, x, z), tensor: 4 (over y_lo, core).
Axes of the slice: x: 4, y: 4 (y_hi: 2, y_lo: 2; y = y_hi * 2 + y_lo), z: 4, core: 2. Of those that a mesh axis runs over, the one named last changes fastest.
Arguments:
- hidden_in: bfloat16 [16384, 2048], P('dp'), may hold values from -6 to 6
- cotangent: bfloat16 [16384, 2048], P('dp'), may hold values from -6 to 6
- seq_lengths: int32 [32], replicated, may hold values from 1 to 512, 10240 in all
- slot_order: int32 [32], P('dp'), may hold values from 0 to 31, each once
- attn_gain: bfloat16 [2048], replicated, may hold values from 0.5 to 1.5
- w_query: bfloat16 [2048, 2048], P(None, 'tensor'), may hold values from -0.25 to 0.25
- w_key: bfloat16 [2048, 256], P(None, 'tensor'), may hold values from -0.125 to 0.125
- w_value: bfloat16 [2048, 256], P(None, 'tensor'), may hold values from -0.125 to 0.125
- w_out: bfloat16 [2048, 2048], P('tensor'), may hold values from -0.5 to 0.5
- mlp_gain: bfloat16 [2048], replicated, may hold values from 0.5 to 1.5
- w_gate: bfloat16 [2048, 5632], P(None, 'tensor'), may hold values from -0.125 to 0.125
- w_up: bfloat16 [2048, 5632], P(None, 'tensor'), may hold values from -0.125 to 0.125
- w_down: bfloat16 [5632, 2048], P('tensor'), may hold values from -0.078125 to 0.078125
Outputs:
- output: bfloat16 [16384, 2048], P(('dp', 'tensor'))
- input_grad: float32 [16384, 2048], P(('dp', 'tensor'))
- attn_gain_grad: float32 [2048], replicated
- query_grad: float32 [2048, 2048], P('dp', 'tensor')
- key_grad: float32 [2048, 256], P('dp', 'tensor')
- value_grad: float32 [2048, 256], P('dp', 'tensor')
- out_grad: float32 [2048, 2048], P('tensor', 'dp')
- mlp_gain_grad: float32 [2048], replicated
- gate_grad: float32 [2048, 5632], P('dp', 'tensor')
- up_grad: float32 [2048, 5632], P('dp', 'tensor')
- down_grad: float32 [5632, 2048], P('tensor', 'dp')
Inputs may be any that keep to these rules, and one draw needn't show every extreme that they name: seq_lengths[i] counts the real tokens of sequence i; they sum to 10240 and the largest is exactly 512. Slot s (rows s * 512 to (s + 1) * 512 - 1) holds sequence slot_order[s]; every sequence is held once.
All inputs are finite; a program needn't handle non-finite values.
Results may differ from a plain program's by a relative error of at most 0.014.
Values may be sent and summed in bfloat16 or wider, within the bound.
No kernel may reach another device: no remote copies, remote signals or barrier semaphores. Data moves between devices by JAX's collectives and lax.ppermute only.
A program may use at most 256 MiB of HBM per device.

v0:
```python
import jax
import jax.numpy as jnp
from jax import lax
from jax.sharding import PartitionSpec as P

HDIM = 64


EPS = 1e-05


def swapped(value, axis, bit):
    return lax.ppermute(value, axis, [(i, i ^ 1 << bit) for i in range(lax.axis_size(axis))])


def rope_tables(row_count, head_width):
    half_width = head_width // 2
    position = jnp.arange(row_count, dtype=jnp.float32)[:, None]
    exponent = jnp.arange(half_width, dtype=jnp.float32) * (2.0 / head_width)
    angles = position / jnp.power(10000.0, exponent)[None, :]
    return (jnp.cos(angles)[:, None, :], jnp.sin(angles)[:, None, :])


def rotate(values, cosine_tab, sine_tab):
    half_width = values.shape[-1] // 2
    first_half = values[..., :half_width]
    second_half = values[..., half_width:]
    return jnp.concatenate(
        [
            first_half * cosine_tab - second_half * sine_tab,
            second_half * cosine_tab + first_half * sine_tab,
        ],
        axis=-1,
    )


def unrotate(gradient, cosine_tab, sine_tab):
    half_width = gradient.shape[-1] // 2
    first_half = gradient[..., :half_width]
    second_half = gradient[..., half_width:]
    return jnp.concatenate(
        [
            first_half * cosine_tab + second_half * sine_tab,
            second_half * cosine_tab - first_half * sine_tab,
        ],
        axis=-1,
    )


def normalize(values):
    inv_rms = lax.rsqrt(jnp.mean(values * values, axis=-1, keepdims=True) + EPS)
    return (values * inv_rms, inv_rms)


def norm_back(grad_normed, normed, inv_rms):
    return inv_rms * (grad_normed - normed * jnp.mean(grad_normed * normed, axis=-1, keepdims=True))


def per_device(
    hidden_in,
    cotangent,
    seq_lengths,
    slot_order,
    attn_gain,
    w_query,
    w_key,
    w_value,
    w_out,
    mlp_gain,
    w_gate,
    w_up,
    w_down,
):
    row_count = hidden_in.shape[0]
    head_width = HDIM
    query_heads = w_query.shape[1] // head_width
    own_keys = w_key.shape[1] // head_width
    pair_heads = 2 * own_keys
    group_size = query_heads // pair_heads
    key_cols = own_keys * head_width
    scaling = head_width ** (-0.5)
    share_rows = row_count // lax.axis_size("tensor")
    first_row = lax.axis_index("tensor") * share_rows
    is_even = lax.axis_index("tensor") % 2 == 0
    sequence = slot_order[0]
    length = jnp.sum(
        jnp.where(jnp.arange(seq_lengths.shape[0], dtype=jnp.int32) == sequence, seq_lengths, 0)
    )
    position = jnp.arange(row_count, dtype=jnp.int32)
    live_rows = position < length
    allowed = (position[None, :] <= position[:, None]) & live_rows[None, :]
    cosine_tab, sine_tab = rope_tables(row_count, head_width)
    gain_one = attn_gain.astype(jnp.float32)
    gain_two = mlp_gain.astype(jnp.float32)
    inputs = hidden_in.astype(jnp.float32)
    normed_one, inv_one = normalize(inputs)
    attn_in = (normed_one * gain_one).astype(jnp.bfloat16)
    query_rot = rotate(
        jnp.dot(attn_in, w_query, preferred_element_type=jnp.float32).reshape(
            row_count, query_heads, head_width
        ),
        cosine_tab,
        sine_tab,
    )
    key_rot = rotate(
        jnp.dot(attn_in, w_key, preferred_element_type=jnp.float32).reshape(
            row_count, own_keys, head_width
        ),
        cosine_tab,
        sine_tab,
    )
    queries = query_rot.astype(jnp.bfloat16).reshape(row_count, pair_heads, group_size, head_width)
    key_mine = key_rot.astype(jnp.bfloat16)
    value_mine = (
        jnp.dot(attn_in, w_value, preferred_element_type=jnp.float32)
        .astype(jnp.bfloat16)
        .reshape(row_count, own_keys, head_width)
    )
    packed = jnp.concatenate(
        [key_mine.reshape(row_count, key_cols), value_mine.reshape(row_count, key_cols)], axis=1
    )
    partner = swapped(packed, "tensor", 0)
    key_other = partner[:, :key_cols].reshape(row_count, own_keys, head_width)
    value_other = partner[:, key_cols:].reshape(row_count, own_keys, head_width)
    key_heads = jnp.where(
        is_even,
        jnp.concatenate([key_mine, key_other], axis=1),
        jnp.concatenate([key_other, key_mine], axis=1),
    )
    value_heads = jnp.where(
        is_even,
        jnp.concatenate([value_mine, value_other], axis=1),
        jnp.concatenate([value_other, value_mine], axis=1),
    )

    def masked_scores():
        raw_scores = (
            jnp.einsum("sgqd,tgd->gqst", queries, key_heads, preferred_element_type=jnp.float32)
            * scaling
        )
        return jnp.where(allowed, raw_scores, -1e30)

    masked = masked_scores()
    row_max = jnp.max(masked, axis=-1, keepdims=True)
    exp_scores = jnp.exp(masked - row_max)
    row_total = jnp.sum(exp_scores, axis=-1, keepdims=True)
    lse_kept = row_max + jnp.log(row_total)
    probs_low = (exp_scores / row_total).astype(jnp.bfloat16)
    attended = jnp.einsum(
        "gqst,tgd->sgqd", probs_low, value_heads, preferred_element_type=jnp.float32
    )
    attended = attended.reshape(row_count, query_heads * head_width).astype(jnp.bfloat16)
    attn_part = jnp.dot(attended, w_out, preferred_element_type=jnp.float32)
    middle = inputs + lax.psum(attn_part, "tensor")
    normed_two, inv_two = normalize(middle)
    mlp_in = (normed_two * gain_two).astype(jnp.bfloat16)
    gate_val = (
        jnp.dot(mlp_in, w_gate, preferred_element_type=jnp.float32)
        .astype(jnp.bfloat16)
        .astype(jnp.float32)
    )
    up_val = (
        jnp.dot(mlp_in, w_up, preferred_element_type=jnp.float32)
        .astype(jnp.bfloat16)
        .astype(jnp.float32)
    )
    sigmoid_gate = jax.nn.sigmoid(gate_val)
    activated = gate_val * sigmoid_gate
    hidden = (activated * up_val).astype(jnp.bfloat16)
    mlp_part = jnp.dot(hidden, w_down, preferred_element_type=jnp.float32)
    result = middle + lax.psum(mlp_part.astype(jnp.bfloat16), "tensor").astype(jnp.float32)
    output_rows = lax.dynamic_slice_in_dim(result, first_row, share_rows, 0).astype(jnp.bfloat16)
    grad_out_low = cotangent * live_rows[:, None].astype(jnp.bfloat16)
    grad_out_full = grad_out_low.astype(jnp.float32)
    grad_down = jnp.einsum("sf,sd->fd", hidden, grad_out_low, preferred_element_type=jnp.float32)
    grad_hidden = jnp.einsum("sd,fd->sf", grad_out_low, w_down, preferred_element_type=jnp.float32)
    grad_gate_low = (
        grad_hidden * up_val * sigmoid_gate * (1.0 + gate_val * (1.0 - sigmoid_gate))
    ).astype(jnp.bfloat16)
    grad_up_low = (grad_hidden * activated).astype(jnp.bfloat16)
    grad_gate = jnp.einsum("sd,sf->df", mlp_in, grad_gate_low, preferred_element_type=jnp.float32)
    grad_up = jnp.einsum("sd,sf->df", mlp_in, grad_up_low, preferred_element_type=jnp.float32)
    mlp_back = jnp.einsum("sf,df->sd", grad_gate_low, w_gate, preferred_element_type=jnp.float32)
    mlp_back = mlp_back + jnp.einsum(
        "sf,df->sd", grad_up_low, w_up, preferred_element_type=jnp.float32
    )
    grad_normed_two = lax.psum(mlp_back, "tensor")
    grad_middle = grad_out_full + norm_back(grad_normed_two * gain_two, normed_two, inv_two)
    branch_grad = grad_middle.astype(jnp.bfloat16)
    own_grad_middle = lax.dynamic_slice_in_dim(grad_middle, first_row, share_rows, 0)
    gain_two_part = jnp.sum(
        lax.dynamic_slice_in_dim(grad_normed_two * normed_two, first_row, share_rows, 0), axis=0
    )
    grad_attn_out = jnp.einsum(
        "sh,sd->hd", attended, branch_grad, preferred_element_type=jnp.float32
    )
    grad_attended = jnp.einsum(
        "sd,hd->sh", branch_grad, w_out, preferred_element_type=jnp.float32
    ).astype(jnp.bfloat16)
    grad_attended = grad_attended.reshape(row_count, pair_heads, group_size, head_width)
    probs_again = jnp.where(allowed, jnp.exp(masked_scores() - lse_kept), 0.0)
    probs_again_low = probs_again.astype(jnp.bfloat16)
    grad_probs = jnp.einsum(
        "sgqd,tgd->gqst", grad_attended, value_heads, preferred_element_type=jnp.float32
    )
    grad_values = jnp.einsum(
        "gqst,sgqd->tgd", probs_again_low, grad_attended, preferred_element_type=jnp.float32
    )
    row_delta = jnp.sum(grad_probs * probs_again, axis=-1, keepdims=True)
    grad_scores = (probs_again * (grad_probs - row_delta)).astype(jnp.bfloat16)
    grad_queries = (
        jnp.einsum("gqst,tgd->sgqd", grad_scores, key_heads, preferred_element_type=jnp.float32)
        * scaling
    )
    grad_keys = (
        jnp.einsum("gqst,sgqd->tgd", grad_scores, queries, preferred_element_type=jnp.float32)
        * scaling
    )
    keys_first = grad_keys[:, :own_keys]
    keys_second = grad_keys[:, own_keys:]
    values_first = grad_values[:, :own_keys]
    values_second = grad_values[:, own_keys:]
    keys_kept = jnp.where(is_even, keys_first, keys_second)
    keys_sent = jnp.where(is_even, keys_second, keys_first)
    values_kept = jnp.where(is_even, values_first, values_second)
    values_sent = jnp.where(is_even, values_second, values_first)
    outgoing = jnp.concatenate(
        [keys_sent.reshape(row_count, key_cols), values_sent.reshape(row_count, key_cols)], axis=1
    )
    incoming = swapped(outgoing, "tensor", 0)
    key_total = keys_kept + incoming[:, :key_cols].reshape(row_count, own_keys, head_width)
    value_total = values_kept + incoming[:, key_cols:].reshape(row_count, own_keys, head_width)
    query_low = unrotate(
        grad_queries.reshape(row_count, query_heads, head_width), cosine_tab, sine_tab
    ).astype(jnp.bfloat16)
    query_low = query_low.reshape(row_count, query_heads * head_width)
    key_low = (
        unrotate(key_total, cosine_tab, sine_tab).astype(jnp.bfloat16).reshape(row_count, key_cols)
    )
    value_low = value_total.astype(jnp.bfloat16).reshape(row_count, key_cols)
    grad_query = jnp.einsum("sd,sh->dh", attn_in, query_low, preferred_element_type=jnp.float32)
    grad_key = jnp.einsum("sd,sh->dh", attn_in, key_low, preferred_element_type=jnp.float32)
    grad_value = jnp.einsum("sd,sh->dh", attn_in, value_low, preferred_element_type=jnp.float32)
    attn_back = jnp.einsum("sh,dh->sd", query_low, w_query, preferred_element_type=jnp.float32)
    attn_back = attn_back + jnp.einsum(
        "sh,dh->sd", key_low, w_key, preferred_element_type=jnp.float32
    )
    attn_back = attn_back + jnp.einsum(
        "sh,dh->sd", value_low, w_value, preferred_element_type=jnp.float32
    )
    grad_normed_one = lax.psum(attn_back, "tensor")
    own_normed_grad = lax.dynamic_slice_in_dim(grad_normed_one, first_row, share_rows, 0)
    own_normed_one = lax.dynamic_slice_in_dim(normed_one, first_row, share_rows, 0)
    own_inv_one = lax.dynamic_slice_in_dim(inv_one, first_row, share_rows, 0)
    input_grad = own_grad_middle + norm_back(
        own_normed_grad * gain_one, own_normed_one, own_inv_one
    )
    gain_one_part = jnp.sum(own_normed_grad * own_normed_one, axis=0)
    gain_one_grad, gain_two_grad = lax.psum((gain_one_part, gain_two_part), ("dp", "tensor"))
    summed = (
        lax.psum_scatter(grad_query, "dp", scatter_dimension=0, tiled=True),
        lax.psum_scatter(grad_key, "dp", scatter_dimension=0, tiled=True),
        lax.psum_scatter(grad_value, "dp", scatter_dimension=0, tiled=True),
        lax.psum_scatter(grad_attn_out, "dp", scatter_dimension=1, tiled=True),
        lax.psum_scatter(grad_gate, "dp", scatter_dimension=0, tiled=True),
        lax.psum_scatter(grad_up, "dp", scatter_dimension=0, tiled=True),
        lax.psum_scatter(grad_down, "dp", scatter_dimension=1, tiled=True),
    )
    return (
        output_rows,
        input_grad,
        gain_one_grad,
        summed[0],
        summed[1],
        summed[2],
        summed[3],
        gain_two_grad,
        summed[4],
        summed[5],
        summed[6],
    )


def solution(mesh):
    return jax.shard_map(
        per_device,
        mesh=mesh,
        in_specs=(
            P("dp", None),
            P("dp", None),
            P(),
            P("dp"),
            P(),
            P(None, "tensor"),
            P(None, "tensor"),
            P(None, "tensor"),
            P("tensor", None),
            P(),
            P(None, "tensor"),
            P(None, "tensor"),
            P("tensor", None),
        ),
        out_specs=(
            P(("dp", "tensor"), None),
            P(("dp", "tensor"), None),
            P(),
            P("dp", "tensor"),
            P("dp", "tensor"),
            P("dp", "tensor"),
            P("tensor", "dp"),
            P(),
            P("dp", "tensor"),
            P("dp", "tensor"),
            P("tensor", "dp"),
        ),
        check_vma=False,
    )
```

profile of v0, /device:TPU:1, one launch (start us, length us, event | category | flops | bytes accessed | tf_op | source)
XLA Modules:
  0.0 1773.1 jit_solution(6624400763423112596)
XLA Ops:
  17.7 3.6 fusion.70
  33.8 91.5 %all-reduce.6.cloned.1.call-done = f32[512,2048]{1,0:T(8,128)} async-done(((f32[512,2048]{1,0:T(8,128)}), f32[512,2048]{1,0:T(8,128)}) %all-reduce.6.cloned.1.call-update) | async-done | bytes 4194320 | tf_op jit(solution)/shard_map/psum | solution.py:154
  125.3 5.5 multiply_reduce_fusion.1
  135.0 8.0 convolution_convert_fusion.1
  143.1 4.6 convolution_convert_fusion
  147.7 6.1 fusion.13
  157.3 5.3 convolution_add_fusion
  164.2 8.5 convolution_convert_fusion.2
  172.8 82.4 %all-reduce.10.cloned.1.call-done = f32[512,2048]{1,0:T(8,128)} async-done(((f32[512,2048]{1,0:T(8,128)}), f32[512,2048]{1,0:T(8,128)}) %all-reduce.10.cloned.1.call-update) | async-done | bytes 4194320 | tf_op jit(solution)/shard_map/psum | solution.py:187
  255.2 4.1 multiply_reduce_fusion
  259.9 4.3 multiply_add_fusion
  286.8 5.5 fusion.30
  297.6 8.8 fusion.67
  306.4 7.6 fusion.75
  315.6 8.2 fusion.18
  328.0 83.1 %all-reduce.12.cloned.1.call-done = f32[512,2048]{1,0:T(8,128)} async-done(((f32[512,2048]{1,0:T(8,128)}), f32[512,2048]{1,0:T(8,128)}) %all-reduce.12.cloned.1.call-update) | async-done | bytes 4194320 | tf_op jit(solution)/shard_map/psum | solution.py:251
  412.9 66.8 %all-reduce = (f32[2048]{0:T(1024)}, f32[2048]{0:T(1024)}) all-reduce(f32[2048]{0:T(1024)S(1)} %get-tuple-element.11, f32[2048]{0:T(1024)S(1)} %fusion.28), channel_id=1, replica_groups=mesh['dp'=32,'tensor'=4] {'dp','tensor'}, use_global_device_ids=true, to_apply=%region_13.14 | all-reduce | flops 4096 | bytes 32768 | tf_op jit(solution)/shard_map/psum | solution.py:259
  482.8 91.8 %reduce-scatter.10.cloned.1.call-done = f32[64,64]{1,0:T(8,128)} async-done(((f32[2048,64]{1,0:T(8,128)}), f32[64,64]{1,0:T(8,128)}) %reduce-scatter.10.cloned.1.call-update) | async-done | bytes 16400 | tf_op jit(solution)/shard_map/reduce_scatter | solution.py:262
  574.6 182.7 %reduce-scatter.12.cloned.1.call-done = f32[64,64]{1,0:T(8,128)} async-done(((f32[2048,64]{1,0:T(8,128)}), f32[64,64]{1,0:T(8,128)}) %reduce-scatter.12.cloned.1.call-update) | async-done | bytes 16400 | tf_op jit(solution)/shard_map/reduce_scatter | solution.py:263
  757.4 192.3 %reduce-scatter.14.cloned.1.call-done = f32[512,64]{0,1:T(8,128)} async-done(((f32[512,2048]{0,1:T(8,128)}), f32[512,64]{0,1:T(8,128)}) %reduce-scatter.14.cloned.1.call-update) | async-done | bytes 131088 | tf_op jit(solution)/shard_map/reduce_scatter | solution.py:264
  949.7 189.9 %reduce-scatter.8.cloned.1.call-done = f32[64,512]{1,0:T(8,128)} async-done(((f32[2048,512]{1,0:T(8,128)}), f32[64,512]{1,0:T(8,128)}) %reduce-scatter.8.cloned.1.call-update) | async-done | bytes 131088 | tf_op jit(solution)/shard_map/reduce_scatter | solution.py:261
  1139.5 208.9 %reduce-scatter.18.cloned.1.call-done = f32[64,1408]{1,0:T(8,128)} async-done(((f32[2048,1408]{1,0:T(8,128)}), f32[64,1408]{1,0:T(8,128)}) %reduce-scatter.18.cloned.1.call-update) | async-done | bytes 360464 | tf_op jit(solution)/shard_map/reduce_scatter | solution.py:266
  1348.5 208.2 %reduce-scatter.16.cloned.1.call-done = f32[64,1408]{1,0:T(8,128)} async-done(((f32[2048,1408]{1,0:T(8,128)}), f32[64,1408]{1,0:T(8,128)}) %reduce-scatter.16.cloned.1.call-update) | async-done | bytes 360464 | tf_op jit(solution)/shard_map/reduce_scatter | solution.py:265
  1556.7 209.4 %reduce-scatter.20.cloned.1.call-done = f32[1408,64]{0,1:T(8,128)} async-done(((f32[1408,2048]{0,1:T(8,128)}), f32[1408,64]{0,1:T(8,128)}) %reduce-scatter.20.cloned.1.call-update) | async-done | bytes 360464 | tf_op jit(solution)/shard_map/reduce_scatter | solution.py:267
  (183 shorter events, 70.1 us)
Async XLA Ops:
  7.2 21.0 %copy-start = (bf16[512,2048]{1,0:T(8,128)(2,1)S(1)}, bf16[512,2048]{1,0:T(8,128)(2,1)}, u32[]{:S(2)}) copy-start(bf16[512,2048]{1,0:T(8,128)(2,1)} %param.21) | copy-start | bytes 6291460
  7.2 118.1 %all-reduce.6.cloned.1.call-start = ((), (), s32[]{:S(2)}) async-start(), calls=%async_computation.7 | async-start | bytes 8388608 | tf_op jit(solution)/shard_map/psum | solution.py:154
  7.3 8.2 copy-start.34
  9.5 8.2 copy-start.30
  12.7 8.7 copy-start.17
  13.9 7.7 collective-permute-start
  31.4 223.8 %all-reduce.10.cloned.1.call-start = ((), (), s32[]{:S(2)}) async-start(), calls=%async_computation.9 | async-start | bytes 8388608 | tf_op jit(solution)/shard_map/psum | solution.py:187
  130.8 12.2 slice-start.4
  135.0 8.0 copy-start.8
  135.0 8.0 slice-start.5
  135.0 12.7 slice-start.6
  143.1 10.8 slice-start.2
  162.6 161.3 %all-reduce.8.cloned.1.call-start = ((), (), s32[]{:S(2)}) async-start(), calls=%async_computation.8 | async-start | bytes 4194304 | tf_op jit(solution)/shard_map/psum | solution.py:171
  172.8 238.4 %all-reduce.12.cloned.1.call-start = ((), (), s32[]{:S(2)}) async-start(), calls=%async_computation.10 | async-start | bytes 8388608 | tf_op jit(solution)/shard_map/psum | solution.py:251
  255.2 10.9 slice-start
  275.0 2.1 collective-permute-start.1
  281.1 293.6 %reduce-scatter.10.cloned.1.call-start = ((), (), s32[]{:S(2)}) async-start(), calls=%async_computation.12 | async-start | bytes 1081344 | tf_op jit(solution)/shard_map/reduce_scatter | solution.py:262
  284.7 472.7 %reduce-scatter.12.cloned.1.call-start = ((), (), s32[]{:S(2)}) async-start(), calls=%async_computation.13 | async-start | bytes 1081344 | tf_op jit(solution)/shard_map/reduce_scatter | solution.py:263
  286.7 663.0 %reduce-scatter.14.cloned.1.call-start = ((), (), s32[]{:S(2)}) async-start(), calls=%async_computation.14 | async-start | bytes 4325376 | tf_op jit(solution)/shard_map/reduce_scatter | solution.py:264
  292.3 847.3 %reduce-scatter.8.cloned.1.call-start = ((), (), s32[]{:S(2)}) async-start(), calls=%async_computation.11 | async-start | bytes 4325376 | tf_op jit(solution)/shard_map/reduce_scatter | solution.py:261
  295.9 1052.6 %reduce-scatter.18.cloned.1.call-start = ((), (), s32[]{:S(2)}) async-start(), calls=%async_computation.16 | async-start | bytes 11894784 | tf_op jit(solution)/shard_map/reduce_scatter | solution.py:266
  306.4 1250.3 %reduce-scatter.16.cloned.1.call-start = ((), (), s32[]{:S(2)}) async-start(), calls=%async_computation.15 | async-start | bytes 11894784 | tf_op jit(solution)/shard_map/reduce_scatter | solution.py:265
  314.0 1452.1 %reduce-scatter.20.cloned.1.call-start = ((), (), s32[]{:S(2)}) async-start(), calls=%async_computation.17 | async-start | bytes 11894784 | tf_op jit(solution)/shard_map/reduce_scatter | solution.py:267
  323.9 1442.2 %copy-start.1 = (bf16[512,2048]{1,0:T(8,128)(2,1)S(1)}, bf16[512,2048]{1,0:T(8,128)(2,1)}, u32[]{:S(2)}) copy-start(bf16[512,2048]{1,0:T(8,128)(2,1)} %param.21) | copy-start | bytes 6291460
  (40 other events, 135.1 us)
Sparse Core Ops, SparseCore 0:
  31.5 93.7 all-reduce.5
  162.7 92.4 all-reduce.9
  257.7 58.2 all-reduce.7
  318.6 92.4 all-reduce.11
  413.9 160.6 reduce-scatter.9
  577.5 179.7 reduce-scatter.11
  760.3 189.3 reduce-scatter.13
  952.6 186.8 reduce-scatter.7
  1142.5 205.8 reduce-scatter.17
  1351.3 205.3 reduce-scatter.15
  1559.7 206.3 reduce-scatter.19
where the time goes:
time: 1800 us; the launch traced here: 1770 us
  waiting for transfers between devices  1540 us (86%)
  matrix products  98.9 us (5%)
  blocking collectives  66.8 us (4%)
  other arithmetic  38.2 us (2%)
    reduce_scatter x1, waiting for transfers between devices, per_device(): lax.psum_scatter(grad_down, 'dp', scatter_dimension=1, tiled=True)  209 us
    reduce_scatter x1, waiting for transfers between devices, per_device(): lax.psum_scatter(grad_up, 'dp', scatter_dimension=0, tiled=True)  209 us
    reduce_scatter x1, waiting for transfers between devices, per_device(): lax.psum_scatter(grad_gate, 'dp', scatter_dimension=0, tiled=True)  208 us
    reduce_scatter x1, waiting for transfers between devices, per_device(): lax.psum_scatter(grad_attn_out, 'dp', scatter_dimension=1, tiled=True)  192 us
    reduce_scatter x1, waiting for transfers between devices, per_device(): lax.psum_scatter(grad_query, 'dp', scatter_dimension=0, tiled=True)  190 us
    reduce_scatter x1, waiting for transfers between devices, per_device(): lax.psum_scatter(grad_value, 'dp', scatter_dimension=0, tiled=True)  183 us
    reduce_scatter x1, waiting for transfers between devices, per_device(): lax.psum_scatter(grad_key, 'dp', scatter_dimension=0, tiled=True)  91.8 us
    psum x1, waiting for transfers between devices, per_device(): middle = inputs + lax.psum(attn_part, 'tensor')  91.5 us
  transfers between devices with their start and end apart: 13, of which 10 were waited for; matrix products, arithmetic and copies ran while one was open for 5% of the time, Pallas kernels for 0%

commit v1 on v0

v1 whole, which is shorter than its diff:
```python
import functools

import jax
import jax.numpy as jnp
from jax import lax
from jax.experimental import pallas as pl
from jax.experimental.pallas import tpu as pltpu
from jax.sharding import PartitionSpec as P

HDIM = 64
EPS = 1e-05
LOW = jnp.bfloat16
FULL = jnp.float32


def ring_perm(ring, bits):
    step = bits * (4 if ring == "x" else 1)
    return [(i, i ^ step) for i in range(32)]


def over_ring(value, ring, bits):
    return lax.ppermute(value, "dp", ring_perm(ring, bits))


def over_yh(value):
    return lax.ppermute(value, "dp", [(i, i ^ 16) for i in range(32)])


def over_tensor(value, bits):
    return lax.ppermute(value, "tensor", [(i, i ^ bits) for i in range(4)])


def dot(a, b):
    return jnp.dot(a, b, preferred_element_type=FULL)


def dot_t(a, b):
    return lax.dot_general(a, b, (((1,), (1,)), ((), ())), preferred_element_type=FULL)


def rotate(values, cosine_tab, sine_tab, sign):
    half_width = values.shape[-1] // 2
    first_half = values[..., :half_width]
    second_half = values[..., half_width:]
    return jnp.concatenate(
        [
            first_half * cosine_tab - sign * second_half * sine_tab,
            second_half * cosine_tab + sign * first_half * sine_tab,
        ],
        axis=-1,
    )


def dot_rows(a, b):
    return lax.dot_general(a, b, (((0,), (0,)), ((), ())), preferred_element_type=FULL)


def wgrad_body(n_src, crossed, ring, order, where, *refs):
    sides, fans = refs[:n_src], refs[n_src : 2 * n_src]
    send_ref, keep_ref, total = refs[2 * n_src :]
    value = dot_rows(sides[0][...], fans[0][...])
    for side, fan in zip(sides[1:], fans[1:]):
        if crossed:
            value = value + dot_rows(side[:256], fan[256:]) + dot_rows(side[256:], fan[:256])
        else:
            value = value + dot_rows(side[...], fan[...])
    total[...] = value

    def piece(bits):
        start = pl.multiple_of(where[8 + bits], 64)
        return total[pl.ds(start, 64), :].astype(LOW)

    if ring == "z":
        send_ref[0:64] = piece(order[0])
        send_ref[64:128] = piece(order[1])
        keep_ref[0:64] = piece(order[2])
        keep_ref[64:128] = piece(order[3])
    else:
        step = pl.program_id(0)

        @pl.when(step < 2)
        def _():
            for bits in range(4):
                send_ref[64 * bits : 64 * bits + 64] = piece(bits)

        @pl.when(step >= 2)
        def _():
            for bits in range(4):
                keep_ref[64 * bits : 64 * bits + 64] = piece(bits)


def wgrad(place, half_at, sides, fans, ring, first, crossed=False):
    n_src = len(sides)
    width = fans[0].shape[1]
    x, z = place
    order = (first, 2, 0, 4 - first)
    if ring == "x":
        steps = [x ^ bits for bits in order]
    else:
        steps = [x ^ bits for bits in range(4)]
    whole = [half_at * 4 + step for step in steps]
    pieces = [(z ^ bits) * 64 for bits in range(4)]
    where = jnp.stack(steps + whole + pieces).astype(jnp.int32)
    tokens = sides[0].shape[0]

    def side_spec(side):
        shift = 4 if side.shape[1] == 2048 else 0
        return pl.BlockSpec((tokens, 256), lambda i, where: (0, where[shift + i]))

    in_specs = [side_spec(side) for side in sides]
    in_specs += [pl.BlockSpec((tokens, width), lambda i, where: (0, 0)) for _ in fans]
    if ring == "x":
        out_specs = [
            pl.BlockSpec((256, width), lambda i, where: (jnp.minimum(i, 1), 0)),
            pl.BlockSpec((256, width), lambda i, where: (jnp.maximum(i - 2, 0), 0)),
        ]
    else:
        out_specs = [pl.BlockSpec((128, width), lambda i, where: (i, 0))] * 2
    send, keep = pl.pallas_call(
        functools.partial(wgrad_body, n_src, crossed, ring, order),
        grid_spec=pltpu.PrefetchScalarGridSpec(
            num_scalar_prefetch=1,
            grid=(4,),
            in_specs=in_specs,
            out_specs=out_specs,
            scratch_shapes=[pltpu.VMEM((256, width), FULL)],
        ),
        out_shape=[jax.ShapeDtypeStruct((512, width), LOW)] * 2,
        compiler_params=pltpu.CompilerParams(
            vmem_limit_bytes=40 * 1024 * 1024, dimension_semantics=("arbitrary",)
        ),
        cost_estimate=pl.CostEstimate(
            flops=2 * n_src * tokens * 1024 * width,
            bytes_accessed=2 * n_src * tokens * (1024 + width) + 4 * 1024 * width,
            transcendentals=0,
        ),
    )(where, *sides, *fans)
    return send, keep


def scatter_ring(send, keep, ring, first):
    width = send.shape[1]
    shape = (4, 2, 64, width) if ring == "z" else (2, 4, 64, width)
    axis = 1 if ring == "z" else 0
    got = over_ring(send, ring, first).reshape(shape)
    keep = keep.reshape(shape)

    def part(which):
        mine = lax.index_in_dim(keep, which, axis, False).astype(FULL)
        return mine + lax.index_in_dim(got, which, axis, False).astype(FULL)

    got_next = over_ring(part(1).astype(LOW), ring, 4 - first)
    return part(0) + got_next.astype(FULL)


def scatter_blocks(value, ring, first):
    send = jnp.stack([value[first], value[2]]).astype(LOW)
    got = over_ring(send, ring, first).astype(FULL)
    got_next = over_ring((value[4 - first] + got[1]).astype(LOW), ring, 4 - first)
    return value[0] + got[0] + got_next.astype(FULL)


def scatter_yh(first_half, second_half, same):
    keep = jnp.where(same, first_half, second_half)
    send = jnp.where(same, second_half, first_half).astype(LOW)
    return keep + over_yh(send).astype(FULL)


def regroup(total, ring, at):
    parts = [total[0]]
    for bits in (1, 2, 3):
        parts.append(over_ring(total[bits].astype(LOW), ring, bits).astype(FULL))
    low_bit, high_bit = (at & 1) == 1, (at & 2) == 2
    a, b, c, d = parts
    a, b, c, d = (
        jnp.where(low_bit, b, a),
        jnp.where(low_bit, a, b),
        jnp.where(low_bit, d, c),
        jnp.where(low_bit, c, d),
    )
    a, b, c, d = (
        jnp.where(high_bit, c, a),
        jnp.where(high_bit, d, b),
        jnp.where(high_bit, a, c),
        jnp.where(high_bit, b, d),
    )
    return jnp.concatenate([a, b, c, d], axis=1)


def gather_side(value, core, ring):
    mine = lax.dynamic_slice_in_dim(value, core * 1024, 1024, 1)
    near = [over_ring(mine, ring, bits) for bits in (1, 3, 2)]
    far = [over_tensor(part, 1) for part in near]
    return near, far


def spread_columns(value, ring, at):
    width = value.shape[1] // 4
    out = [lax.dynamic_slice_in_dim(value, at * width, width, 1)]
    for bits in (1, 3, 2):
        part = lax.dynamic_slice_in_dim(value, (at ^ bits) * width, width, 1)
        out.append(over_ring(part, ring, bits))
    return out


def grouped_grad(place, core, yh, side, gathered, fan, ring):
    x, z = place
    at = x if ring == "x" else z
    other = "z" if ring == "x" else "x"
    near, far = gathered
    fans = spread_columns(fan, ring, at)
    halves = []
    for half, (sides, first) in enumerate([(near, 1), (far, 3)]):
        half_at = core ^ half
        send, keep = wgrad(place, half_at, [side] + sides, fans, other, first, half == 1)
        halves.append(scatter_ring(send, keep, other, first))
    total = scatter_yh(halves[0], halves[1], yh == core)
    return regroup(total, ring, at)


def plain_grad(place, core, yh, side, fan, ring):
    other = "z" if ring == "x" else "x"
    halves = []
    for half, first in enumerate([1, 3]):
        send, keep = wgrad(place, core ^ half, [side], [fan], ring, first)
        value = scatter_ring(send, keep, ring, first)
        halves.append(scatter_blocks(value, other, first))
    return scatter_yh(halves[0], halves[1], yh == core)


def scatter_rows(part):
    got = over_tensor(part(256, 512).astype(LOW), 1).astype(FULL)
    mine = part(0, 256)
    got_next = over_tensor((mine[128:] + got[128:]).astype(LOW), 2)
    return mine[:128] + got[:128] + got_next.astype(FULL)


def gather_rows(own):
    pair = jnp.concatenate([own, over_tensor(own, 2)], axis=0)
    return jnp.concatenate([pair, over_tensor(pair, 1)], axis=0)


def sum_everywhere(value):
    for ring in ("x", "z"):
        value = value + over_ring(value, ring, 1) + over_ring(value, ring, 2) + over_ring(value, ring, 3)
    value = value + over_yh(value)
    value = value + over_tensor(value, 2)
    return value + over_tensor(value, 1)


def per_device(
    hidden_in,
    cotangent,
    seq_lengths,
    slot_order,
    attn_gain,
    w_query,
    w_key,
    w_value,
    w_out,
    mlp_gain,
    w_gate,
    w_up,
    w_down,
):
    rows = hidden_in.shape[0]
    own_rows = rows // 4
    heads = w_query.shape[1] // HDIM
    group = heads // 2
    ff = w_gate.shape[1]
    scaling = HDIM ** (-0.5)
    dp_at = lax.axis_index("dp")
    yh, x, z = dp_at // 16, (dp_at // 4) % 4, dp_at % 4
    place = (x, z)
    tensor_at = lax.axis_index("tensor")
    core = tensor_at % 2
    is_even = core == 0
    blocks = [tensor_at ^ bits for bits in (0, 2, 1, 3)]

    def reorder(value):
        return jnp.concatenate(
            [lax.dynamic_slice_in_dim(value, at * own_rows, own_rows, 0) for at in blocks], axis=0
        )

    sequence = slot_order[0]
    length = jnp.sum(
        jnp.where(jnp.arange(seq_lengths.shape[0], dtype=jnp.int32) == sequence, seq_lengths, 0)
    )
    position = jnp.concatenate(
        [at * own_rows + jnp.arange(own_rows, dtype=jnp.int32) for at in blocks]
    )
    live_rows = position < length
    live = live_rows[:, None].astype(FULL)
    allowed = (position[None, :] <= position[:, None]) & live_rows[None, :]
    half_width = HDIM // 2
    exponent = jnp.arange(half_width, dtype=FULL) * (2.0 / HDIM)
    angles = position.astype(FULL)[:, None] / jnp.power(10000.0, exponent)[None, :]
    cosine_tab, sine_tab = jnp.cos(angles)[:, None, :], jnp.sin(angles)[:, None, :]
    gain_one = attn_gain.astype(FULL)
    gain_two = mlp_gain.astype(FULL)

    dy_low = reorder(cotangent)
    dy_gathered = gather_side(dy_low, core, "z")

    hidden_rows = reorder(hidden_in)
    inputs = hidden_rows.astype(FULL)
    inv_one = lax.rsqrt(jnp.mean(inputs * inputs, axis=-1, keepdims=True) + EPS)
    attn_in = (inputs * inv_one * gain_one).astype(LOW)

    query_rot = rotate(
        dot(attn_in, w_query).reshape(rows, heads, HDIM), cosine_tab, sine_tab, 1.0
    )
    queries = query_rot.astype(LOW).reshape(rows, 2, group, HDIM)
    key_value = dot(attn_in, jnp.concatenate([w_key, w_value], axis=1))
    key_mine = rotate(key_value[:, None, :HDIM], cosine_tab, sine_tab, 1.0)[:, 0].astype(LOW)
    value_mine = key_value[:, HDIM:].astype(LOW)
    packed = jnp.concatenate([key_mine, value_mine], axis=1)
    partner = over_tensor(packed, 1)
    partner = jnp.concatenate([partner[2 * own_rows :], partner[: 2 * own_rows]], axis=0)
    first = jnp.where(is_even, packed, partner)
    second = jnp.where(is_even, partner, packed)
    both = jnp.stack([first, second], axis=1)
    key_heads, value_heads = both[..., :HDIM], both[..., HDIM:]

    def masked_scores():
        raw_scores = (
            jnp.einsum("sgqd,tgd->gqst", queries, key_heads, preferred_element_type=FULL)
            * scaling
        )
        return jnp.where(allowed, raw_scores, -1e30)

    masked = masked_scores()
    row_max = jnp.max(masked, axis=-1, keepdims=True)
    exp_scores = jnp.exp(masked - row_max)
    row_total = jnp.sum(exp_scores, axis=-1, keepdims=True)
    lse_kept = row_max + jnp.log(row_total)
    probs_low = (exp_scores / row_total).astype(LOW)
    attended = jnp.einsum("gqst,tgd->sgqd", probs_low, value_heads, preferred_element_type=FULL)
    attended = attended.reshape(rows, heads * HDIM).astype(LOW)

    attn_sum = scatter_rows(lambda a, b: dot(attended[a:b], w_out))
    middle = inputs[:own_rows] + attn_sum
    inv_two = lax.rsqrt(jnp.mean(middle * middle, axis=-1, keepdims=True) + EPS)
    normed_two = middle * inv_two
    mlp_in = gather_rows((normed_two * gain_two).astype(LOW))
    mlp_gathered = gather_side(mlp_in, core, "x")

    gate_val = dot(mlp_in, w_gate).astype(LOW).astype(FULL)
    up_val = dot(mlp_in, w_up).astype(LOW).astype(FULL)
    sigmoid_gate = jax.nn.sigmoid(gate_val)
    activated = gate_val * sigmoid_gate
    hidden = (activated * up_val).astype(LOW)
    hidden_live = jnp.where(live_rows[:, None], hidden, jnp.zeros_like(hidden))
    grad_hidden = dot_t(dy_low, w_down) * live
    grad_gate = (
        grad_hidden * up_val * sigmoid_gate * (1.0 + gate_val * (1.0 - sigmoid_gate))
    ).astype(LOW)
    grad_up = (grad_hidden * activated).astype(LOW)

    down_pad = jnp.pad(hidden_live, ((0, 0), (0, 1536 - ff)))
    down_rows = grouped_grad(place, core, yh, dy_low, dy_gathered, down_pad, "z")

    mlp_back = scatter_rows(
        lambda a, b: dot_t(grad_gate[a:b], w_gate) + dot_t(grad_up[a:b], w_up)
    )
    gate_up = jnp.concatenate(
        [grad_gate, grad_up, jnp.zeros((rows, 3072 - 2 * ff), LOW)], axis=1
    )
    gate_up_rows = grouped_grad(place, core, yh, mlp_in, mlp_gathered, gate_up, "x")

    mlp_out = scatter_rows(lambda a, b: dot(hidden[a:b], w_down))
    output_rows = (middle + mlp_out).astype(LOW)

    scaled_two = mlp_back * gain_two
    dmid = dy_low[:own_rows].astype(FULL) * live[:own_rows] + inv_two * (
        scaled_two - normed_two * jnp.mean(scaled_two * normed_two, axis=-1, keepdims=True)
    )
    gain_two_part = jnp.sum(mlp_back * normed_two, axis=0)
    dmid_low = gather_rows(dmid.astype(LOW))

    out_rows = plain_grad(place, core, yh, dmid_low, attended, "z")

    grad_attended = dot_t(dmid_low, w_out).astype(LOW).reshape(rows, 2, group, HDIM)
    probs_again = jnp.where(allowed, jnp.exp(masked_scores() - lse_kept), 0.0)
    probs_again_low = probs_again.astype(LOW)
    grad_probs = jnp.einsum(
        "sgqd,tgd->gqst", grad_attended, value_heads, preferred_element_type=FULL
    )
    grad_values = jnp.einsum(
        "gqst,sgqd->tgd", probs_again_low, grad_attended, preferred_element_type=FULL
    )
    row_delta = jnp.sum(grad_probs * probs_again, axis=-1, keepdims=True)
    grad_scores = (probs_again * (grad_probs - row_delta)).astype(LOW)
    grad_queries = (
        jnp.einsum("gqst,tgd->sgqd", grad_scores, key_heads, preferred_element_type=FULL)
        * scaling
    )
    grad_keys = (
        jnp.einsum("gqst,sgqd->tgd", grad_scores, queries, preferred_element_type=FULL) * scaling
    )
    grad_both = jnp.concatenate([grad_keys, grad_values], axis=2)
    kept = jnp.where(is_even, grad_both[:, 0], grad_both[:, 1])
    sent = jnp.where(is_even, grad_both[:, 1], grad_both[:, 0])
    incoming = over_tensor(sent, 1)
    key_value_total = kept + jnp.concatenate(
        [incoming[2 * own_rows :], incoming[: 2 * own_rows]], axis=0
    )
    query_low = rotate(
        grad_queries.reshape(rows, heads, HDIM), cosine_tab, sine_tab, -1.0
    ).astype(LOW)
    query_low = query_low.reshape(rows, heads * HDIM)
    key_low = rotate(key_value_total[:, None, :HDIM], cosine_tab, sine_tab, -1.0)[:, 0].astype(LOW)
    key_value_low = jnp.concatenate([key_low, key_value_total[:, HDIM:].astype(LOW)], axis=1)
    qkv_low = jnp.concatenate([query_low, key_value_low], axis=1)

    front = plain_grad(place, core, yh, attn_in, qkv_low[:, :384], "z")
    back = plain_grad(place, core, yh, attn_in, qkv_low[:, 384:], "x")
    qkv_rows = jnp.concatenate([front, back], axis=1)

    w_key_value = jnp.concatenate([w_key, w_value], axis=1)
    attn_back = scatter_rows(
        lambda a, b: dot_t(query_low[a:b], w_query) + dot_t(key_value_low[a:b], w_key_value)
    )
    normed_one = inputs[:own_rows] * inv_one[:own_rows]
    scaled_one = attn_back * gain_one
    input_grad = dmid + inv_one[:own_rows] * (
        scaled_one - normed_one * jnp.mean(scaled_one * normed_one, axis=-1, keepdims=True)
    )
    gain_one_part = jnp.sum(attn_back * normed_one, axis=0)
    gains = sum_everywhere(jnp.stack([gain_one_part, gain_two_part]))
    q_cols = heads * HDIM
    return (
        output_rows,
        input_grad,
        gains[0],
        qkv_rows[:, :q_cols],
        qkv_rows[:, q_cols : q_cols + HDIM],
        qkv_rows[:, q_cols + HDIM :],
        out_rows.T,
        gains[1],
        gate_up_rows[:, :ff],
        gate_up_rows[:, ff : 2 * ff],
        down_rows[:, :ff].T,
    )


def solution(mesh):
    return jax.shard_map(
        per_device,
        mesh=mesh,
        in_specs=(
            P("dp", None),
            P("dp", None),
            P(),
            P("dp"),
            P(),
            P(None, "tensor"),
            P(None, "tensor"),
            P(None, "tensor"),
            P("tensor", None),
            P(),
            P(None, "tensor"),
            P(None, "tensor"),
            P("tensor", None),
        ),
        out_specs=(
            P(("dp", "tensor"), None),
            P(("dp", "tensor"), None),
            P(),
            P("dp", "tensor"),
            P("dp", "tensor"),
            P("dp", "tensor"),
            P("tensor", "dp"),
            P(),
            P("dp", "tensor"),
            P("dp", "tensor"),
            P("tensor", "dp"),
        ),
        check_vma=False,
    )
```

time: 1800 us -> 504 us (0.28)
  waiting for transfers between devices: 1540 us -> 209 us
  starting transfers between devices: 3.4 us -> 107 us
  blocking collectives: 66.8 us -> 0 us
  matrix products: 98.9 us -> 57.6 us
  Pallas kernels: 0 us -> 36.6 us
    reduce_scatter x7 -> x0, waiting for transfers between devices: 1280 us -> none  [the longest x1 209 us: per_device(): lax.psum_scatter(grad_down, 'dp', scatter_dimension=1, tiled=True)]
    psum x4 -> x0, waiting for transfers between devices: 257 us -> none  [the longest x1 91.5 us: per_device(): middle = inputs + lax.psum(attn_part, 'tensor')]
    ppermute x2 -> x84, waiting for transfers between devices: 0.01 us -> 209 us  [the longest x56 175 us: over_ring(): return lax.ppermute(value, 'dp', ring_perm(ring, bits))]
    ppermute x2 -> x84, starting transfers between devices: 2.06 us -> 107 us  [the longest x56 54.8 us: over_ring(): return lax.ppermute(value, 'dp', ring_perm(ring, bits))]
    psum x1 -> x0, blocking collectives: 66.8 us -> none  [per_device(): lax.psum((gain_one_part, gain_two_part), ('dp', 'tensor'))]
    dot_general x22 -> x19, matrix products: 91.2 us -> 48.5 us  [the longest x10 25.3 us: dot_t(): lax.dot_general(a, b, (((1,), (1,)), ((), ())), preferred_element_type=FULL)]
    pallas_call x0 -> x10, Pallas kernels: none -> 36.6 us  [wgrad(): pl.pallas_call(functools.partial(wgrad_body, n_src, crossed, ring, order)...]
  transfers between devices with their start and end apart: 13 -> 84, of which waited for: 10 -> 33; matrix products, arithmetic and copies ran while one was open for 5% -> 21% of each run, Pallas kernels for 0% -> 7%
where the time goes in v1:
time: 504 us; the launch traced here: 495 us
  waiting for transfers between devices  209 us (41%)
  starting transfers between devices  107 us (21%)
  matrix products  57.6 us (11%)
  other arithmetic  53.5 us (11%)
  Pallas kernels  36.6 us (7%)
  local copies, waits for them, and re-layouts  26.1 us (5%)
    ppermute x56, waiting for transfers between devices, over_ring(): return lax.ppermute(value, 'dp', ring_perm(ring, bits))  175 us
    ppermute x56, starting transfers between devices, over_ring(): return lax.ppermute(value, 'dp', ring_perm(ring, bits))  54.8 us
    ppermute x22, starting transfers between devices, over_tensor(): return lax.ppermute(value, 'tensor', [(i, i ^ bits) for i in range(4)])  41.9 us
    pallas_call x10, Pallas kernels, wgrad(): pl.pallas_call(functools.partial(wgrad_body, n_src, crossed, ring, order)...  36.6 us
    ppermute x22, waiting for transfers between devices, over_tensor(): return lax.ppermute(value, 'tensor', [(i, i ^ bits) for i in range(4)])  32.1 us
    dot_general x10, matrix products, dot_t(): lax.dot_general(a, b, (((1,), (1,)), ((), ())), preferred_element_type=FULL)  25.3 us
    dot_general x8, matrix products, dot(): return jnp.dot(a, b, preferred_element_type=FULL)  20.7 us
    unnamed x183, local copies, waits for them, and re-layouts  11.1 us
  transfers between devices with their start and end apart: 84, of which 33 were waited for; matrix products, arithmetic and copies ran while one was open for 21% of the time, Pallas kernels for 7%

profile of v1, /device:TPU:1, one launch (start us, length us, event | category | flops | bytes accessed | tf_op | source)
XLA Modules:
  0.0 494.5 jit_solution(10481241217488517516)
XLA Ops:
  35.6 11.4 %collective-permute-done.2 = bf16[128,2048]{1,0:T(8,128)(2,1)S(1)} collective-permute-done((bf16[128,2048]{1,0:T(8,128)(2,1)S(1)}, bf16[128,2048]{1,0:T(8,128)(2,1)S(1)}, u32[]{:S(2)}, u32[]{:S(2)}) %collective-permute-start.2) | collective-permute-done | bytes 524320 | tf_op jit(solution)/shard_map/ppermute | solution.py:30
  68.7 11.5 %collective-permute-done.67.refs_1_ = bf16[512,1024]{1,0:T(8,128)(2,1)S(1)} collective-permute-done((bf16[512,1024]{1,0:T(8,128)(2,1)}, bf16[512,1024]{1,0:T(8,128)(2,1)S(1)}, u32[]{:S(2)}, u32[]{:S(2)}) %collective-permute-start.67) | collective-permute-done | bytes 1048608 | tf_op jit(solution)/shard_map/ppermute | solution.py:22
  80.2 3.5 collective-permute-start.75
  83.7 19.9 %collective-permute-done.68.refs_2_ = bf16[512,1024]{1,0:T(8,128)(2,1)} collective-permute-done((bf16[512,1024]{1,0:T(8,128)(2,1)}, bf16[512,1024]{1,0:T(8,128)(2,1)}, u32[]{:S(2)}, u32[]{:S(2)}) %collective-permute-start.68) | collective-permute-done | bytes 1048608 | tf_op jit(solution)/shard_map/ppermute | solution.py:22
  108.0 6.7 %convolution_convert_fusion.1 = bf16[512,1408]{1,0:T(8,128)(2,1)S(1)} fusion(bf16[2048,1408]{1,0:T(8,128)(2,1)} %param.23, bf16[256,2048]{1,0:T(8,128)(2,1)} %collective-permute-done.4, bf16[128,2048]{1,0:T(8,128)(2,1)} %collective-permute-done.3, bf16[128,2048]{1,0:T(8,128)(2,1)} %multiply_convert_fusion.2), kind=kOutput, calls=%fused_computation.24 | convolution fusion | flops 2959802368 | bytes 9306112 | tf_op jit(solution)/shard_map/dot_general | solution.py:34
  114.8 6.7 %broadcast_select_fusion = (bf16[512,1408]{1,0:T(8,128)(2,1)S(1)}, bf16[512,1408]{1,0:T(8,128)(2,1)}, bf16[512,1408]{1,0:T(8,128)(2,1)S(1)}) fusion(pred[512]{0:T(512)(128)(4,1)S(1)} %copy-done.74, bf16[512,1408]{1,0:T(8,128)(2,1)S(1)} %convolution_convert_fusion.1, bf16[2048,1408]{1,0:T(8,128)(2,1)S(1)} %bitcast.474, ...), kind=kOutput, calls=%fused_computation.46 | convolution fusion | flops 2966290432 | bytes 13632000 | tf_op jit(solution)/shard_map/dot_general | solution.py:34
  121.6 7.2 %multiply_convert_fusion.1 = (bf16[512,1408]{1,0:T(8,128)(2,1)S(1)}, bf16[512,1408]{1,0:T(8,128)(2,1)S(1)}) fusion(bf16[512,1408]{1,0:T(8,128)(2,1)S(1)} %convolution_convert_fusion.1, bf16[512,1408]{1,0:T(8,128)(2,1)S(1)} %get-tuple-element.154, f32[512]{0:T(512)S(1)} %copy-done.75, bf16[1408,2048]{1,0:T(8,128)(2,1)} %param.25, ...), kind=kOutput, calls=%fused_computation.33 | convolution fusion | flops 2972712960 | bytes 13633536 | tf_op jit(solution)/shard_map/dot_general | solution.py:38
  143.3 4.7 fusion.17
  155.9 5.2 %collective-permute-done.72.refs_7_ = bf16[512,384]{1,0:T(8,128)(2,1)S(1)} collective-permute-done((bf16[512,384]{1,0:T(8,128)(2,1)S(1)}, bf16[512,384]{1,0:T(8,128)(2,1)S(1)}, u32[]{:S(2)}, u32[]{:S(2)}) %collective-permute-start.72) | collective-permute-done | bytes 393248 | tf_op jit(solution)/shard_map/ppermute | solution.py:22
  161.1 4.4 shard_map.221
  168.0 5.3 %shard_map.220 = (bf16[512,384]{1,0:T(8,128)(2,1)S(1)}, bf16[512,384]{1,0:T(8,128)(2,1)S(1)}) custom-call(s32[12]{0:T(128)S(1)} %stack.87.where, bf16[512,2048]{1,0:T(8,128)(2,1)S(1)} %copy-done.5, bf16[512,1024]{1,0:T(8,128)(2,1)S(1)} %collective-permute-done.67.refs_1_, bf16[512,1024]{1,0:T(8,128)(2,1)} %collective-permute-done.68.refs_2_, ...), custom_call_target="tpu_custom_call" | custom-call | flops 1610612736 | bytes 7340032 | tf_op jit(solution)/shard_map/pallas_call | solution.py:119
  176.9 4.9 collective-permute-done.73
  183.8 24.7 %collective-permute-done.79 = bf16[4,64,384]{2,1,0:T(8,128)(2,1)S(1)} collective-permute-done((bf16[4,64,384]{2,1,0:T(8,128)(2,1)S(1)}, bf16[4,64,384]{2,1,0:T(8,128)(2,1)S(1)}, u32[]{:S(2)}, u32[]{:S(2)}) %collective-permute-start.79) | collective-permute-done | bytes 196640 | tf_op jit(solution)/shard_map/ppermute | solution.py:22
  212.8 6.0 %collective-permute-done.6 = bf16[128,2048]{1,0:T(8,128)(2,1)S(1)} collective-permute-done((bf16[128,2048]{1,0:T(8,128)(2,1)S(1)}, bf16[128,2048]{1,0:T(8,128)(2,1)S(1)}, u32[]{:S(2)}, u32[]{:S(2)}) %collective-permute-start.6) | collective-permute-done | bytes 524320 | tf_op jit(solution)/shard_map/ppermute | solution.py:30
  222.3 67.4 %collective-permute-done.54.refs_6_ = bf16[512,768]{1,0:T(8,128)(2,1)S(1)} collective-permute-done((bf16[512,768]{1,0:T(8,128)(2,1)S(1)}, bf16[512,768]{1,0:T(8,128)(2,1)S(1)}, u32[]{:S(2)}, u32[]{:S(2)}) %collective-permute-start.54) | collective-permute-done | bytes 786464 | tf_op jit(solution)/shard_map/ppermute | solution.py:22
  294.9 6.2 %shard_map.218 = (bf16[512,768]{1,0:T(8,128)(2,1)}, bf16[512,768]{1,0:T(8,128)(2,1)S(1)}) custom-call(s32[12]{0:T(128)S(1)} %stack.79.where, bf16[512,2048]{1,0:T(8,128)(2,1)S(1)} %pad_maximum_fusion.refs_0_, bf16[512,1024]{1,0:T(8,128)(2,1)S(1)} %collective-permute-done.50.refs_1_, bf16[512,1024]{1,0:T(8,128)(2,1)S(1)} %collective-permute-done.51.refs_2_, ...), custom_call_target="tpu_custom_call" | custom-call | flops 3221225472 | bytes 10485760 | tf_op jit(solution)/shard_map/pallas_call | solution.py:119
  303.4 5.4 %collective-permute-done.9 = bf16[128,2048]{1,0:T(8,128)(2,1)S(1)} collective-permute-done((bf16[128,2048]{1,0:T(8,128)(2,1)S(1)}, bf16[128,2048]{1,0:T(8,128)(2,1)S(1)}, u32[]{:S(2)}, u32[]{:S(2)}) %collective-permute-start.9) | collective-permute-done | bytes 524320 | tf_op jit(solution)/shard_map/ppermute | solution.py:30
  314.6 6.2 %shard_map.219 = (bf16[512,768]{1,0:T(8,128)(2,1)}, bf16[512,768]{1,0:T(8,128)(2,1)S(1)}) custom-call(s32[12]{0:T(128)S(1)} %stack.85.where, bf16[512,2048]{1,0:T(8,128)(2,1)S(1)} %pad_maximum_fusion.refs_0_, bf16[512,1024]{1,0:T(8,128)(2,1)S(1)} %collective-permute-done.58.refs_1_, bf16[512,1024]{1,0:T(8,128)(2,1)S(1)} %collective-permute-done.59.refs_2_, ...), custom_call_target="tpu_custom_call" | custom-call | flops 3221225472 | bytes 10485760 | tf_op jit(solution)/shard_map/pallas_call | solution.py:119
  330.0 12.4 %collective-permute-done.61 = bf16[512,768]{1,0:T(8,128)(2,1)} collective-permute-done((bf16[512,768]{1,0:T(8,128)(2,1)}, bf16[512,768]{1,0:T(8,128)(2,1)}, u32[]{:S(2)}, u32[]{:S(2)}) %collective-permute-start.61) | collective-permute-done | bytes 786464 | tf_op jit(solution)/shard_map/ppermute | solution.py:22
  393.7 8.4 %collective-permute-done.36 = bf16[512,256]{1,0:T(8,128)(2,1)S(1)} collective-permute-done((bf16[512,256]{1,0:T(8,128)(2,1)S(1)}, bf16[512,256]{1,0:T(8,128)(2,1)S(1)}, u32[]{:S(2)}, u32[]{:S(2)}) %collective-permute-start.36) | collective-permute-done | bytes 262176 | tf_op jit(solution)/shard_map/ppermute | solution.py:22
  423.8 3.7 collective-permute-done.25
  428.2 3.6 collective-permute-done.38
  450.6 5.3 %collective-permute-done.13 = bf16[128,2048]{1,0:T(8,128)(2,1)S(1)} collective-permute-done((bf16[128,2048]{1,0:T(8,128)(2,1)S(1)}, bf16[128,2048]{1,0:T(8,128)(2,1)S(1)}, u32[]{:S(2)}, u32[]{:S(2)}) %collective-permute-start.13) | collective-permute-done | bytes 524320 | tf_op jit(solution)/shard_map/ppermute | solution.py:30
  477.2 15.2 %collective-permute-start.22 = (f32[2,2048]{1,0:T(2,128)S(1)}, f32[2,2048]{1,0:T(2,128)S(1)}, u32[]{:S(2)}, u32[]{:S(2)}) collective-permute-start(f32[2,2048]{1,0:T(2,128)S(1)} %add.592), channel_id=1, source_target_pairs={{0,1},{1,0},{2,3},{3,2},{4,5},{5,4},{6,7},{7,6},{8,9},{9,8},{10,11... | collective-permute-start | bytes 49160 | tf_op jit(solution)/shard_map/ppermute | solution.py:30
  (510 shorter events, 234.3 us)
Async XLA Ops:
  57.8 45.8 %collective-permute-start.68 = (bf16[512,1024]{1,0:T(8,128)(2,1)}, bf16[512,1024]{1,0:T(8,128)(2,1)}, u32[]{:S(2)}, u32[]{:S(2)}) collective-permute-start(bf16[512,1024]{1,0:T(8,128)(2,1)} %constant_dynamic-slice_fusion), channel_id=1, source_target_pairs={{0,12},{4,8},{8,4},{12,0},{16,28},{20,24},{24,20},{28,16},{32,44},... | collective-permute-start | bytes 3145736 | tf_op jit(solution)/shard_map/ppermute | solution.py:22
  60.0 46.2 %collective-permute-start.69 = (bf16[512,1024]{1,0:T(8,128)(2,1)}, bf16[512,1024]{1,0:T(8,128)(2,1)}, u32[]{:S(2)}, u32[]{:S(2)}) collective-permute-start(bf16[512,1024]{1,0:T(8,128)(2,1)} %constant_dynamic-slice_fusion), channel_id=1, source_target_pairs={{0,8},{4,12},{8,0},{12,4},{16,24},{20,28},{24,16},{28,20},{32,40},... | collective-permute-start | bytes 3145736 | tf_op jit(solution)/shard_map/ppermute | solution.py:22
  64.4 43.6 %collective-permute-start.4 = (bf16[256,2048]{1,0:T(8,128)(2,1)}, bf16[256,2048]{1,0:T(8,128)(2,1)}, u32[]{:S(2)}, u32[]{:S(2)}) collective-permute-start(bf16[256,2048]{1,0:T(8,128)(2,1)} %pad_maximum_fusion.3), channel_id=1, source_target_pairs={{0,1},{1,0},{2,3},{3,2},{4,5},{5,4},{6,7},{7,6},{8,9},{9,8},{10,11... | collective-permute-start | bytes 3145736 | tf_op jit(solution)/shard_map/ppermute | solution.py:30
  80.2 69.7 %collective-permute-start.75 = (bf16[512,1024]{1,0:T(8,128)(2,1)S(1)}, bf16[512,1024]{1,0:T(8,128)(2,1)S(1)}, u32[]{:S(2)}, u32[]{:S(2)}) collective-permute-start(bf16[512,1024]{1,0:T(8,128)(2,1)S(1)} %collective-permute-done.67.refs_1_), channel_id=1, source_target_pairs={{0,1},{1,0},{2,3},{3,2},{4,5},{5,4},{6,7},{7,6},{8,9},{9,8},{10,11... | collective-permute-start | bytes 3145736 | tf_op jit(solution)/shard_map/ppermute | solution.py:30
  103.6 49.8 %collective-permute-start.76 = (bf16[512,1024]{1,0:T(8,128)(2,1)}, bf16[512,1024]{1,0:T(8,128)(2,1)S(1)}, u32[]{:S(2)}, u32[]{:S(2)}) collective-permute-start(bf16[512,1024]{1,0:T(8,128)(2,1)} %collective-permute-done.68.refs_2_), channel_id=1, source_target_pairs={{0,1},{1,0},{2,3},{3,2},{4,5},{5,4},{6,7},{7,6},{8,9},{9,8},{10,11... | collective-permute-start | bytes 3145736 | tf_op jit(solution)/shard_map/ppermute | solution.py:30
  106.2 48.5 %collective-permute-start.77 = (bf16[512,1024]{1,0:T(8,128)(2,1)}, bf16[512,1024]{1,0:T(8,128)(2,1)S(1)}, u32[]{:S(2)}, u32[]{:S(2)}) collective-permute-start(bf16[512,1024]{1,0:T(8,128)(2,1)} %collective-permute-done.69.refs_3_), channel_id=1, source_target_pairs={{0,1},{1,0},{2,3},{3,2},{4,5},{5,4},{6,7},{7,6},{8,9},{9,8},{10,11... | collective-permute-start | bytes 3145736 | tf_op jit(solution)/shard_map/ppermute | solution.py:30
  153.4 58.6 %collective-permute-start.53 = (bf16[512,768]{1,0:T(8,128)(2,1)}, bf16[512,768]{1,0:T(8,128)(2,1)S(1)}, u32[]{:S(2)}, u32[]{:S(2)}) collective-permute-start(bf16[512,768]{1,0:T(8,128)(2,1)} %get-tuple-element.82), channel_id=1, source_target_pairs={{0,16},{4,20},{8,24},{12,28},{16,0},{20,4},{24,8},{28,12},{32,48},... | collective-permute-start | bytes 2359304 | tf_op jit(solution)/shard_map/ppermute | solution.py:22
  154.7 28.5 %collective-permute-start.5 = (bf16[256,2048]{1,0:T(8,128)(2,1)S(1)}, bf16[256,2048]{1,0:T(8,128)(2,1)S(1)}, u32[]{:S(2)}, u32[]{:S(2)}) collective-permute-start(bf16[256,2048]{1,0:T(8,128)(2,1)S(1)} %convolution_convert_fusion.3), channel_id=1, source_target_pairs={{0,1},{1,0},{2,3},{3,2},{4,5},{5,4},{6,7},{7,6},{8,9},{9,8},{10,11... | collective-permute-start | bytes 3145736 | tf_op jit(solution)/shard_map/ppermute | solution.py:30
  175.4 116.8 %collective-permute-start.50 = (bf16[512,1024]{1,0:T(8,128)(2,1)S(1)}, bf16[512,1024]{1,0:T(8,128)(2,1)S(1)}, u32[]{:S(2)}, u32[]{:S(2)}) collective-permute-start(bf16[512,1024]{1,0:T(8,128)(2,1)S(1)} %constant_dynamic-slice_fusion.5), channel_id=1, source_target_pairs={{0,16},{4,20},{8,24},{12,28},{16,0},{20,4},{24,8},{28,12},{32,48},... | collective-permute-start | bytes 3145736 | tf_op jit(solution)/shard_map/ppermute | solution.py:22
  181.8 26.7 %collective-permute-start.79 = (bf16[4,64,384]{2,1,0:T(8,128)(2,1)S(1)}, bf16[4,64,384]{2,1,0:T(8,128)(2,1)S(1)}, u32[]{:S(2)}, u32[]{:S(2)}) collective-permute-start(bf16[4,64,384]{2,1,0:T(8,128)(2,1)S(1)} %bitcast.456), channel_id=1, source_target_pairs={{0,16},{4,20},{8,24},{12,28},{16,0},{20,4},{24,8},{28,12},{32,48},... | collective-permute-start | bytes 589832 | tf_op jit(solution)/shard_map/ppermute | solution.py:22
  182.0 26.7 %collective-permute-start.74 = (bf16[4,64,384]{2,1,0:T(8,128)(2,1)S(1)}, bf16[4,64,384]{2,1,0:T(8,128)(2,1)S(1)}, u32[]{:S(2)}, u32[]{:S(2)}) collective-permute-start(bf16[4,64,384]{2,1,0:T(8,128)(2,1)S(1)} %bitcast.457), channel_id=1, source_target_pairs={{0,48},{4,52},{8,56},{12,60},{16,32},{20,36},{24,40},{28,44},{32,1... | collective-permute-start | bytes 589832 | tf_op jit(solution)/shard_map/ppermute | solution.py:22
  208.5 85.9 %collective-permute-start.51 = (bf16[512,1024]{1,0:T(8,128)(2,1)S(1)}, bf16[512,1024]{1,0:T(8,128)(2,1)S(1)}, u32[]{:S(2)}, u32[]{:S(2)}) collective-permute-start(bf16[512,1024]{1,0:T(8,128)(2,1)S(1)} %constant_dynamic-slice_fusion.5), channel_id=1, source_target_pairs={{0,48},{4,52},{8,56},{12,60},{16,32},{20,36},{24,40},{28,44},{32,1... | collective-permute-start | bytes 3145736 | tf_op jit(solution)/shard_map/ppermute | solution.py:22
  209.4 85.1 %collective-permute-start.52 = (bf16[512,1024]{1,0:T(8,128)(2,1)S(1)}, bf16[512,1024]{1,0:T(8,128)(2,1)S(1)}, u32[]{:S(2)}, u32[]{:S(2)}) collective-permute-start(bf16[512,1024]{1,0:T(8,128)(2,1)S(1)} %constant_dynamic-slice_fusion.5), channel_id=1, source_target_pairs={{0,32},{4,36},{8,40},{12,44},{16,48},{20,52},{24,56},{28,60},{32,0... | collective-permute-start | bytes 3145736 | tf_op jit(solution)/shard_map/ppermute | solution.py:22
  212.0 77.7 %collective-permute-start.54 = (bf16[512,768]{1,0:T(8,128)(2,1)S(1)}, bf16[512,768]{1,0:T(8,128)(2,1)S(1)}, u32[]{:S(2)}, u32[]{:S(2)}) collective-permute-start(bf16[512,768]{1,0:T(8,128)(2,1)S(1)} %copy-done.51), channel_id=1, source_target_pairs={{0,48},{4,52},{8,56},{12,60},{16,32},{20,36},{24,40},{28,44},{32,1... | collective-permute-start | bytes 2359304 | tf_op jit(solution)/shard_map/ppermute | solution.py:22
  218.8 76.1 %collective-permute-start.55 = (bf16[512,768]{1,0:T(8,128)(2,1)S(1)}, bf16[512,768]{1,0:T(8,128)(2,1)S(1)}, u32[]{:S(2)}, u32[]{:S(2)}) collective-permute-start(bf16[512,768]{1,0:T(8,128)(2,1)S(1)} %copy-done.50), channel_id=1, source_target_pairs={{0,32},{4,36},{8,40},{12,44},{16,48},{20,52},{24,56},{28,60},{32,0... | collective-permute-start | bytes 2359304 | tf_op jit(solution)/shard_map/ppermute | solution.py:22
  301.1 26.2 %collective-permute-start.56 = (bf16[512,768]{1,0:T(8,128)(2,1)}, bf16[512,768]{1,0:T(8,128)(2,1)}, u32[]{:S(2)}, u32[]{:S(2)}) collective-permute-start(bf16[512,768]{1,0:T(8,128)(2,1)} %get-tuple-element.44), channel_id=1, source_target_pairs={{0,4},{4,0},{8,12},{12,8},{16,20},{20,16},{24,28},{28,24},{32,36},... | collective-permute-start | bytes 2359304 | tf_op jit(solution)/shard_map/ppermute | solution.py:22
  313.1 31.6 %collective-permute-start.10 = (bf16[256,2048]{1,0:T(8,128)(2,1)}, bf16[256,2048]{1,0:T(8,128)(2,1)}, u32[]{:S(2)}, u32[]{:S(2)}) collective-permute-start(bf16[256,2048]{1,0:T(8,128)(2,1)} %pad_maximum_fusion.4), channel_id=1, source_target_pairs={{0,1},{1,0},{2,3},{3,2},{4,5},{5,4},{6,7},{7,6},{8,9},{9,8},{10,11... | collective-permute-start | bytes 3145736 | tf_op jit(solution)/shard_map/ppermute | solution.py:30
  329.2 49.2 %collective-permute-start.57 = (bf16[4,64,768]{2,1,0:T(8,128)(2,1)}, bf16[4,64,768]{2,1,0:T(8,128)(2,1)}, u32[]{:S(2)}, u32[]{:S(2)}) collective-permute-start(bf16[4,64,768]{2,1,0:T(8,128)(2,1)} %fusion.45), channel_id=1, source_target_pairs={{0,12},{4,8},{8,4},{12,0},{16,28},{20,24},{24,20},{28,16},{32,44},... | collective-permute-start | bytes 1179656 | tf_op jit(solution)/shard_map/ppermute | solution.py:22
  344.3 34.1 %collective-permute-start.62 = (bf16[4,64,768]{2,1,0:T(8,128)(2,1)}, bf16[4,64,768]{2,1,0:T(8,128)(2,1)}, u32[]{:S(2)}, u32[]{:S(2)}) collective-permute-start(bf16[4,64,768]{2,1,0:T(8,128)(2,1)} %fusion.46), channel_id=1, source_target_pairs={{0,4},{4,0},{8,12},{12,8},{16,20},{20,16},{24,28},{28,24},{32,36},... | collective-permute-start | bytes 1179656 | tf_op jit(solution)/shard_map/ppermute | solution.py:22
  366.2 37.2 %collective-permute-start.45 = (bf16[512,512]{1,0:T(8,128)(2,1)}, bf16[512,512]{1,0:T(8,128)(2,1)}, u32[]{:S(2)}, u32[]{:S(2)}) collective-permute-start(bf16[512,512]{1,0:T(8,128)(2,1)} %get-tuple-element.42), channel_id=1, source_target_pairs={{0,12},{4,8},{8,4},{12,0},{16,28},{20,24},{24,20},{28,16},{32,44},... | collective-permute-start | bytes 1572872 | tf_op jit(solution)/shard_map/ppermute | solution.py:22
  368.0 41.8 %collective-permute-start.41 = (bf16[512,512]{1,0:T(8,128)(2,1)}, bf16[512,512]{1,0:T(8,128)(2,1)}, u32[]{:S(2)}, u32[]{:S(2)}) collective-permute-start(bf16[512,512]{1,0:T(8,128)(2,1)} %get-tuple-element.40), channel_id=1, source_target_pairs={{0,4},{4,0},{8,12},{12,8},{16,20},{20,16},{24,28},{28,24},{32,36},... | collective-permute-start | bytes 1572872 | tf_op jit(solution)/shard_map/ppermute | solution.py:22
  402.1 44.4 %collective-permute-start.12 = (bf16[256,2048]{1,0:T(8,128)(2,1)S(1)}, bf16[256,2048]{1,0:T(8,128)(2,1)S(1)}, u32[]{:S(2)}, u32[]{:S(2)}) collective-permute-start(bf16[256,2048]{1,0:T(8,128)(2,1)S(1)} %fusion.18), channel_id=1, source_target_pairs={{0,1},{1,0},{2,3},{3,2},{4,5},{5,4},{6,7},{7,6},{8,9},{9,8},{10,11... | collective-permute-start | bytes 3145736 | tf_op jit(solution)/shard_map/ppermute | solution.py:30
  414.6 28.2 %collective-permute-start.46 = (bf16[4,64,512]{2,1,0:T(8,128)(2,1)S(1)}, bf16[4,64,512]{2,1,0:T(8,128)(2,1)S(1)}, u32[]{:S(2)}, u32[]{:S(2)}) collective-permute-start(bf16[4,64,512]{2,1,0:T(8,128)(2,1)S(1)} %fusion.49), channel_id=1, source_target_pairs={{0,4},{4,0},{8,12},{12,8},{16,20},{20,16},{24,28},{28,24},{32,36},... | collective-permute-start | bytes 786440 | tf_op jit(solution)/shard_map/ppermute | solution.py:22
  414.9 30.1 %collective-permute-start.42 = (bf16[4,64,512]{2,1,0:T(8,128)(2,1)S(1)}, bf16[4,64,512]{2,1,0:T(8,128)(2,1)S(1)}, u32[]{:S(2)}, u32[]{:S(2)}) collective-permute-start(bf16[4,64,512]{2,1,0:T(8,128)(2,1)S(1)} %fusion.48), channel_id=1, source_target_pairs={{0,12},{4,8},{8,4},{12,0},{16,28},{20,24},{24,20},{28,16},{32,44},... | collective-permute-start | bytes 786440 | tf_op jit(solution)/shard_map/ppermute | solution.py:22
  (151 other events, 1421.3 us)
